TPU v7x, 32 devices: a whole 2x2x4 slice. The times are simulated.
32 devices in a mesh: mode: 4 (over x, core), member: 8 (over z, y).
Axes of the slice: x: 2, y: 2, z: 4, core: 2. Of those that a mesh axis runs over, the one named last changes fastest.
Arguments:
- ground_accel: bfloat16 [4, 639], replicated, may hold values from -6 to 6
- modal_kernel: bfloat16 [4096, 512], P(('mode', 'member')), may hold values from -0.25 to 0.25
- mode_shapes: bfloat16 [49152, 4096], P('member', 'mode'), may hold values from -0.09375 to 0.09375
- member_owner: int32 [8192, 1], P('member'), may hold values from 0 to 31; in each aligned block of 256 rows (0 to 255, 256 to 511, ...) at most 16 rows name the same one
- member_group: int32 [8192, 1], P('member'), may hold values from 0 to 3
- record_table: int32 [128, 8], P(('mode', 'member')), may hold values from 0 to 3
- case_coef: float32 [8, 6], replicated, may hold values from -1.5 to 1.5
- gravity: float32 [128, 8], P(('mode', 'member')), may hold values from -10 to 10
Outputs:
- demand: float32 [128, 8], P(('mode', 'member'))
Inputs may be any that keep to these rules, and one draw needn't show every extreme that they name: `member_owner`: in each aligned block of 1024 / 4 members no owner is named more than 16 times, a bound that some block reaches.
All inputs are finite; a program needn't handle non-finite values.
Results may differ from a plain program's by a relative error of at most 0.0065.
Values may be sent and summed in bfloat16 or wider, within the bound.
A program may use at most 64 MiB of HBM per device.

v0:
```python
import jax
import jax.numpy as jnp
from jax import lax
from jax.sharding import PartitionSpec as P


def lagged_table(ground_accel, tap_count):
    record_count, span_len = ground_accel.shape
    step_count = span_len - tap_count + 1
    offsets = tap_count - 1 + jnp.arange(step_count)[None, :] - jnp.arange(tap_count)[:, None]
    lag_table = ground_accel[:, offsets]
    return jnp.transpose(lag_table, (1, 0, 2)).reshape(tap_count, record_count * step_count)


def local(
    ground_accel,
    modal_kernel,
    mode_shapes,
    member_owner,
    member_group,
    record_table,
    case_coef,
    gravity,
):
    tap_count = modal_kernel.shape[1]
    record_count = ground_accel.shape[0]
    comp_count = case_coef.shape[1]
    group_count = gravity.shape[0]
    n_mode = lax.axis_size("mode")
    n_member = lax.axis_size("member")
    lagged = lagged_table(ground_accel, tap_count)
    local_resp = jnp.dot(modal_kernel, lagged, preferred_element_type=jnp.float32).astype(
        jnp.bfloat16
    )
    modal_resp = lax.all_gather(local_resp, "member", axis=0, tiled=True)
    own_rows = mode_shapes.shape[0] // n_mode
    forces = lax.psum_scatter(
        jnp.dot(mode_shapes, modal_resp, preferred_element_type=jnp.float32).astype(jnp.bfloat16),
        "mode",
        scatter_dimension=0,
        tiled=True,
    ).astype(jnp.float32)
    members_here = own_rows // comp_count
    owner_total = n_mode * n_member
    slot_depth = max(2, 2 * members_here // owner_total)
    packed = forces.reshape(members_here, comp_count * forces.shape[1])
    first_row = lax.axis_index("mode") * members_here
    owner_ids = lax.dynamic_slice_in_dim(member_owner[:, 0], first_row, members_here)
    group_ids = lax.dynamic_slice_in_dim(member_group[:, 0], first_row, members_here)
    position = jnp.arange(members_here)
    earlier = (owner_ids[:, None] == owner_ids[None, :]) & (position[None, :] < position[:, None])
    member_rank = jnp.sum(earlier.astype(jnp.int32), axis=1)
    slot_index = owner_ids * slot_depth + member_rank
    slot_total = owner_total * slot_depth
    placement = jnp.arange(slot_total)[:, None] == slot_index[None, :]
    outgoing = jnp.dot(placement.astype(jnp.float32), packed, precision=lax.Precision.HIGHEST)
    slot_labels = jnp.max(jnp.where(placement, group_ids[None, :], -1), axis=1)
    incoming, slot_tags = (
        lax.all_to_all(
            outgoing.reshape(owner_total, slot_depth, -1).astype(jnp.bfloat16),
            ("mode", "member"),
            split_axis=0,
            concat_axis=0,
            tiled=True,
        ).astype(jnp.float32),
        lax.all_to_all(
            slot_labels.reshape(owner_total, slot_depth),
            ("mode", "member"),
            split_axis=0,
            concat_axis=0,
            tiled=True,
        ),
    )
    selector = (jnp.arange(group_count)[:, None] == slot_tags.reshape(-1)[None, :]).astype(
        jnp.float32
    )
    group_sums = jnp.dot(
        selector, incoming.reshape(selector.shape[1], -1), precision=lax.Precision.HIGHEST
    )
    group_sums = group_sums.reshape(group_count, comp_count, record_count, -1)
    case_mix = jnp.einsum("sc,gcrt->gsrt", case_coef, group_sums, precision=lax.Precision.HIGHEST)
    record_pick = (record_table[:, :, None] == jnp.arange(record_count)[None, None, :]).astype(
        jnp.float32
    )
    selected = jnp.sum(record_pick[:, :, :, None] * case_mix, axis=2)
    combined = gravity[:, :, None] + selected
    return jnp.max(jnp.abs(combined), axis=2)


def solution(mesh):
    placed = (
        P(),
        P(("mode", "member"), None),
        P("member", "mode"),
        P("member", None),
        P("member", None),
        P(("mode", "member"), None),
        P(),
        P(("mode", "member"), None),
    )
    return jax.shard_map(
        local, mesh=mesh, in_specs=placed, out_specs=P(("mode", "member"), None), check_vma=False
    )
```

profile of v0, /device:TPU:0, one launch (start us, length us, event | category | flops | bytes accessed | tf_op | source)
XLA Modules:
  0.0 461.5 jit_solution(3680047845573878190)
XLA Ops:
  6.5 0.0 copy-start
  6.5 0.0 all-gather.2.cloned.1.call-start
  6.5 0.9 copy.20
  7.4 0.1 fusion.6
  7.5 227.3 %gather_fusion = bf16[65536,4]{1,0:T(8,128)(2,1)} fusion(bf16[4,639]{0,1:T(8,128)(2,1)S(1)} %copy.20, s32[65536]{0:T(1024)S(1)} %fusion.6), kind=kCustom, calls=%fused_computation | custom fusion | bytes 1310720 | tf_op jit(solution)/shard_map/gather | solution.py:11
  234.9 17.2 %copy.21 = bf16[512,128,4]{0,1,2:T(8,128)(2,1)S(1)} copy(bf16[512,128,4]{2,1,0:T(8,128)(2,1)} %bitcast.41) | data formatting | bytes 1048576 | tf_op jit(solution)/shard_map/gather | solution.py:11
  252.1 0.0 copy-done
  252.1 0.9 fusion.1
  253.1 0.0 all-gather.2.cloned.1.call-update
  253.1 0.0 reduce-scatter.2.cloned.1.call-start
  253.1 42.3 %all-gather.2.cloned.1.call-done = bf16[1024,512]{0,1:T(8,128)(2,1)} async-done(((bf16[128,512]{0,1:T(8,128)(2,1)}), bf16[1024,512]{0,1:T(8,128)(2,1)}) %all-gather.2.cloned.1.call-update) | async-done | bytes 1048592 | tf_op jit(solution)/shard_map/all_gather | solution.py:35
  295.5 11.7 %fusion = bf16[6144,512]{0,1:T(8,128)(2,1)} fusion(bf16[1024,512]{0,1:T(8,128)(2,1)} %all-gather.2.cloned.1.call-done, bf16[6144,1024]{1,0:T(8,128)(2,1)} %param.10), kind=kOutput, calls=%fused_computation.2 | convolution fusion | flops 6445596672 | bytes 19922944 | tf_op jit(solution)/shard_map/dot_general | solution.py:38
  307.1 0.0 reduce-scatter.2.cloned.1.call-update
  307.2 0.7 constant_dynamic-slice_fusion
  307.9 0.2 convert_reduce_fusion
  308.1 0.2 select_reduce_fusion
  308.2 0.7 all_to_all.9
  308.9 3.5 all-to-all-start
  312.4 52.1 %reduce-scatter.2.cloned.1.call-done = bf16[1536,512]{0,1:T(8,128)(2,1)} async-done(((bf16[6144,512]{0,1:T(8,128)(2,1)}), bf16[1536,512]{0,1:T(8,128)(2,1)}) %reduce-scatter.2.cloned.1.call-update) | async-done | bytes 1572880 | tf_op jit(solution)/shard_map/reduce_scatter | solution.py:37
  364.6 1.7 copy.22
  366.3 1.4 reshape.112
  367.7 2.7 convolution_convert_fusion.1
  370.4 0.0 copy-start.1
  370.4 0.0 all-to-all-done
  370.4 4.6 %all-to-all-start.1 = ((bf16[32,16,3072]{2,1,0:T(8,128)(2,1)}), bf16[32,16,3072]{2,1,0:T(8,128)(2,1)S(1)}, u32[]{:S(2)}, u32[]{:S(2)}) async-start(bf16[32,16,3072]{2,1,0:T(8,128)(2,1)} %convolution_convert_fusion.1), calls=%async_computation.2 | async-start | bytes 6291456 | tf_op jit(solution)/shard_map/all_to_all | solution.py:59
  375.0 0.0 copy-done.1
  375.0 0.5 broadcast.73
  375.5 0.7 reduce.3
  376.2 0.1 eq.85
  376.3 71.8 %all-to-all-done.1 = bf16[32,16,3072]{2,1,0:T(8,128)(2,1)S(1)} async-done(((bf16[32,16,3072]{2,1,0:T(8,128)(2,1)}), bf16[32,16,3072]{2,1,0:T(8,128)(2,1)S(1)}, u32[]{:S(2)}, u32[]{:S(2)}) %all-to-all-start.1) | async-done | bytes 3145760 | tf_op jit(solution)/shard_map/all_to_all | solution.py:59
  448.1 2.8 copy.23
  450.9 0.0 copy-start.3
  450.9 0.0 copy-start.2
  450.9 2.8 fusion.13
  453.7 0.0 copy-done.3
  453.7 0.2 fusion.3
  453.9 0.0 copy-done.2
  453.9 0.7 abs_reduce_fusion
  (4 shorter events, 0.0 us)
Async XLA Ops:
  6.5 245.6 %copy-start = (bf16[128,512]{1,0:T(8,128)(2,1)S(1)}, bf16[128,512]{1,0:T(8,128)(2,1)}, u32[]{:S(2)}) copy-start(bf16[128,512]{1,0:T(8,128)(2,1)} %param.9) | copy-start | bytes 393220
  6.5 288.9 %all-gather.2.cloned.1.call-start = ((), (), s32[]{:S(2)}) async-start(), calls=%async_computation.3 | async-start | bytes 1179648 | tf_op jit(solution)/shard_map/all_gather | solution.py:35
  253.1 111.5 %reduce-scatter.2.cloned.1.call-start = ((), (), s32[]{:S(2)}) async-start(), calls=%async_computation.4 | async-start | bytes 7864320 | tf_op jit(solution)/shard_map/reduce_scatter | solution.py:37
  308.9 61.5 %all-to-all-start = ((s32[32,1,16]{2,1,0:T(1,128)}), s32[32,1,16]{2,1,0:T(1,128)S(1)}, u32[]{:S(2)}, u32[]{:S(2)}) async-start(s32[32,1,16]{2,1,0:T(1,128)} %bitcast.2), calls=%async_computation | async-start | bytes 32768 | tf_op jit(solution)/shard_map/all_to_all | solution.py:66
  370.4 4.6 %copy-start.1 = (s32[4,8]{1,0:T(4,128)S(1)}, s32[4,8]{1,0:T(4,128)}, u32[]{:S(2)}) copy-start(s32[4,8]{1,0:T(4,128)} %param.13) | copy-start | bytes 388
  370.4 77.7 %all-to-all-start.1 = ((bf16[32,16,3072]{2,1,0:T(8,128)(2,1)}), bf16[32,16,3072]{2,1,0:T(8,128)(2,1)S(1)}, u32[]{:S(2)}, u32[]{:S(2)}) async-start(bf16[32,16,3072]{2,1,0:T(8,128)(2,1)} %convolution_convert_fusion.1), calls=%async_computation.2 | async-start | bytes 6291456 | tf_op jit(solution)/shard_map/all_to_all | solution.py:59
  450.9 2.8 copy-start.3
  450.9 3.0 copy-start.2
Sparse Core Ops, SparseCore 0:
  253.2 42.2 all-gather.1
  307.3 57.2 reduce-scatter.1
where the time goes:
time: 462 us
  local copies, waits for them, and re-layouts  253 us (55%)
  waiting for transfers between devices  166 us (36%)
  matrix products  18.3 us (4%)
  between operations  13.5 us (3%)
  starting transfers between devices  8.14 us (2%)
    gather x2, local copies, waits for them, and re-layouts, lagged_table(): lag_table = ground_accel[:, offsets]  245 us
    all_to_all x1, waiting for transfers between devices, local(): lax.all_to_all(outgoing.reshape(owner_total, slot_depth, -1).astype(jnp.b...  71.8 us
    reduce_scatter x1, waiting for transfers between devices, local(): lax.psum_scatter(jnp.dot(mode_shapes, modal_resp, preferred_element_type=...  52.1 us
    all_gather x1, waiting for transfers between devices, local(): modal_resp = lax.all_gather(local_resp, 'member', axis=0, tiled=True)  42.3 us
    dot_general x1, matrix products, local(): jnp.dot(mode_shapes, modal_resp, preferred_element_type=jnp.float32)  11.7 us
  transfers between devices with their start and end apart: 4, of which 3 were waited for; matrix products, arithmetic and copies ran while one was open for 2% of the time, Pallas kernels for 0%

commit v1 on v0

v1 whole, which is shorter than its diff:
```python
import functools

import jax
import jax.numpy as jnp
from jax import lax
from jax.experimental import pallas as pl
from jax.experimental.pallas import tpu as pltpu
from jax.sharding import PartitionSpec as P

MESH = pl.DeviceIdType.MESH
BF = jnp.bfloat16
F32 = jnp.float32


def kernel(
    dims,
    accel_ref,
    kern_ref,
    shapes_ref,
    code_ref,
    rec_ref,
    mix_ref,
    grav_ref,
    out_ref,
    mbuf,
    kbuf,
    recbuf,
    acc,
    lagged,
    sums,
    xbuf,
    abuf,
    ybuf,
    bbuf,
    msem,
    loc_sem,
    z_send,
    z_recv,
    y_send,
    y_recv,
    zr_send,
    zr_recv,
    yr_send,
    yr_recv,
    mr_send,
    mr_recv,
    a_send,
    a_recv,
    b_send,
    b_recv,
):
    n_mode, n_member, nz, ny, comps, own_rows = dims
    n_records = accel_ref.shape[0]
    taps = kern_ref.shape[1]
    shard = kern_ref.shape[0]
    n_chunk, chunk = code_ref.shape
    group_rows = acc.shape[0]
    mode = lax.axis_index("mode")
    member = lax.axis_index("member")
    z = member // ny
    y = lax.rem(member, ny)
    slab = n_member * own_rows

    def load(i):
        rows = pl.ds(pl.multiple_of(i * chunk, chunk), chunk)
        return pltpu.make_async_copy(shapes_ref.at[rows, :], mbuf.at[rows, :], msem.at[i])

    for i in range(n_chunk):
        load(i).start()

    def member_at(zz, yy):
        return zz * ny + yy

    def krows(m):
        return pl.ds(pl.multiple_of(m * shard, shard), shard)

    def rrows(b, m):
        return pl.ds(pl.multiple_of((b * n_member + m) * own_rows, own_rows), own_rows)

    own_k = pltpu.make_async_copy(kern_ref, kbuf.at[krows(member), :], loc_sem.at[0])
    own_k.start()
    own_r = pltpu.make_async_copy(rec_ref, recbuf.at[rrows(mode, member), :], loc_sem.at[1])
    own_r.start()

    barrier = pltpu.get_barrier_semaphore()
    for d in range(1, n_member):
        pl.semaphore_signal(
            barrier, inc=1, device_id={"member": lax.rem(member + d, n_member)}, device_id_type=MESH
        )
    for d in range(1, n_mode):
        pl.semaphore_signal(
            barrier, inc=1, device_id={"mode": lax.rem(mode + d, n_mode)}, device_id_type=MESH
        )
    pl.semaphore_wait(barrier, n_member + n_mode - 2)

    def remote(src, dst, send, recv, target):
        return pltpu.make_async_remote_copy(
            src_ref=src,
            dst_ref=dst,
            send_sem=send,
            recv_sem=recv,
            device_id=target,
            device_id_type=MESH,
        )

    sent = []
    z_copies, zr_copies, y_copies, yr_copies = {}, {}, {}, {}

    def send_y(d):
        source = member_at(lax.rem(z + nz - d, nz), y)
        for e in range(1, ny):
            target = {"member": member_at(z, lax.rem(y + e, ny))}
            kr, rr = krows(source), rrows(mode, source)
            ksrc = kern_ref if d == 0 else kbuf.at[kr, :]
            rsrc = rec_ref if d == 0 else recbuf.at[rr, :]
            y_copies[d, e] = remote(
                ksrc, kbuf.at[kr, :], y_send.at[d, e - 1], y_recv.at[d, e - 1], target
            )
            yr_copies[d, e] = remote(
                rsrc, recbuf.at[rr, :], yr_send.at[d, e - 1], yr_recv.at[d, e - 1], target
            )
            yr_copies[d, e].start()
            y_copies[d, e].start()

    for d in range(1, nz):
        target = {"member": member_at(lax.rem(z + d, nz), y)}
        z_copies[d] = remote(
            kern_ref, kbuf.at[krows(member), :], z_send.at[d - 1], z_recv.at[d - 1], target
        )
        zr_copies[d] = remote(
            rec_ref,
            recbuf.at[rrows(mode, member), :],
            zr_send.at[d - 1],
            zr_recv.at[d - 1],
            target,
        )
        zr_copies[d].start()
    send_y(0)
    for d in range(1, nz):
        z_copies[d].start()

    steps = lagged.shape[1] // n_records
    for r in range(n_records):
        for q in range(taps // steps):
            start = taps - steps * (q + 1)
            piece = jnp.broadcast_to(accel_ref[r : r + 1, start : start + 2 * steps], (steps, 2 * steps))
            rolled = pltpu.roll(piece, steps + 1, 1, stride=1, stride_axis=0)
            lagged[q * steps : (q + 1) * steps, r * steps : (r + 1) * steps] = rolled[
                :, :steps
            ].astype(BF)

    acc[...] = jnp.zeros_like(acc)
    part = chunk if group_rows % chunk == 0 else group_rows

    def chunk_step(i, carry):
        load(i).wait()
        code = code_ref[pl.ds(i, 1), :]
        block = mbuf[pl.ds(pl.multiple_of(i * chunk, chunk), chunk), :]

        def row_step(p, inner):
            first = pl.multiple_of(p * part, part)
            rows = lax.broadcasted_iota(jnp.int32, (part, chunk), 0) + first
            hot = jnp.where(rows == code, 1.0, 0.0).astype(BF)
            acc[pl.ds(first, part), :] += jnp.dot(hot, block, preferred_element_type=F32)
            return inner

        return lax.fori_loop(0, group_rows // part, row_step, carry)

    marks = [(n_chunk * (d + 1)) // (nz + 1) for d in range(1, nz)]
    done = 0
    for d in range(1, nz):
        lax.fori_loop(done, marks[d - 1], chunk_step, 0)
        done = marks[d - 1]
        z_copies[d].wait_recv()
        zr_copies[d].wait_recv()
        send_y(d)
    lax.fori_loop(done, n_chunk, chunk_step, 0)

    own_k.wait()
    own_r.wait()
    for d in range(nz):
        for e in range(1, ny):
            yr_copies[d, e].wait_recv()
    mine = pl.ds(pl.multiple_of(mode * slab, slab), slab)
    mr_copies = []
    for d in range(1, n_mode):
        copy = remote(
            recbuf.at[mine, :],
            recbuf.at[mine, :],
            mr_send.at[d - 1],
            mr_recv.at[d - 1],
            {"mode": lax.rem(mode + d, n_mode)},
        )
        copy.start()
        mr_copies.append(copy)
    for d in range(nz):
        for e in range(1, ny):
            y_copies[d, e].wait_recv()

    def contract(p, carry):
        rows = pl.ds(pl.multiple_of(p * part, part), part)
        by_tap = jnp.dot(acc[rows, :].astype(BF), kbuf[...], preferred_element_type=F32)
        sums[rows, :] = jnp.dot(
            by_tap.astype(BF), lagged[...], preferred_element_type=F32
        ).astype(BF)
        return carry

    lax.fori_loop(0, group_rows // part, contract, 0)
    for copy in mr_copies:
        copy.wait_recv()

    mixed_rows, mixed_from = mix_ref.shape[1:]

    def mix_slab(target):
        for k in range(slab // mixed_rows):
            to = pl.ds(
                pl.multiple_of(target * slab + k * mixed_rows, mixed_rows), mixed_rows
            )
            start = (target * (slab // mixed_rows) + k) * mixed_from
            got = sums[pl.ds(pl.multiple_of(start, mixed_from), mixed_from), :]
            mixed = jnp.dot(mix_ref[0], got, preferred_element_type=F32) + jnp.dot(
                mix_ref[1], got, preferred_element_type=F32
            )
            wanted = recbuf[to, :].astype(F32)
            picked = jnp.zeros((mixed_rows, steps), F32)
            for r in range(n_records):
                picked = jnp.where(wanted == r, mixed[:, r * steps : (r + 1) * steps], picked)
            xbuf[to, :] = picked.astype(BF)

    a_copies = []
    for d in range(n_mode - 1, 0, -1):
        target = lax.rem(mode + d, n_mode)
        mix_slab(target)
        copy = remote(
            xbuf.at[pl.ds(pl.multiple_of(target * slab, slab), slab), :],
            abuf.at[d - 1],
            a_send.at[d - 1],
            a_recv.at[d - 1],
            {"mode": target},
        )
        copy.start()
        a_copies.append((d, copy))
    mix_slab(mode)
    total = xbuf[mine, :].astype(F32)
    for d, copy in a_copies:
        copy.wait_recv()
        total = total + abuf[d - 1].astype(F32)
    ybuf[...] = total.astype(BF)

    b_copies = []
    for d in range(1, n_member):
        target = lax.rem(member + d, n_member)
        copy = remote(
            ybuf.at[pl.ds(pl.multiple_of(target * own_rows, own_rows), own_rows), :],
            bbuf.at[d - 1],
            b_send.at[d - 1],
            b_recv.at[d - 1],
            {"member": target},
        )
        copy.start()
        b_copies.append(copy)
    own = ybuf[pl.ds(pl.multiple_of(member * own_rows, own_rows), own_rows), :].astype(F32)
    for d, copy in enumerate(b_copies):
        copy.wait_recv()
        own = own + bbuf[d].astype(F32)
    out_ref[...] = jnp.max(jnp.abs(own + grav_ref[...]), axis=1, keepdims=True)

    for copies in (z_copies, zr_copies, y_copies, yr_copies):
        for copy in copies.values():
            copy.wait_send()
    for copy in mr_copies + b_copies + [c for _, c in a_copies]:
        copy.wait_send()


def local(
    n_mode,
    n_member,
    ground_accel,
    modal_kernel,
    mode_shapes,
    member_owner,
    member_group,
    record_table,
    case_coef,
    gravity,
):
    nz = 4
    ny = n_member // nz
    n_records, span = ground_accel.shape
    shard, taps = modal_kernel.shape
    steps = span - taps + 1
    cases, comps = case_coef.shape
    own_groups = gravity.shape[0]
    own_rows = own_groups * cases
    groups = n_mode * n_member * own_groups
    rows, modes = mode_shapes.shape
    chunk = 128 * comps
    n_chunk = rows // chunk
    group_rows = groups * comps

    accel = jnp.pad(ground_accel.astype(F32), ((0, 0), (0, taps + steps - span)))
    group = (member_owner * own_groups + member_group) * comps
    code = (group + jnp.arange(comps)[None, :]).reshape(n_chunk, chunk)
    rec = jnp.broadcast_to(record_table.astype(BF).reshape(own_rows, 1), (own_rows, steps))
    mix_groups = 32
    mix = jnp.kron(jnp.eye(mix_groups, dtype=F32), case_coef)
    high = mix.astype(BF)
    mix = jnp.stack([high, (mix - high.astype(F32)).astype(BF)])
    grav = gravity.reshape(own_rows, 1)

    vmem = pl.BlockSpec(memory_space=pltpu.VMEM)
    anywhere = pl.BlockSpec(memory_space=pl.ANY)
    dma = pltpu.SemaphoreType.DMA
    slab = n_member * own_rows
    out = pl.pallas_call(
        functools.partial(kernel, (n_mode, n_member, nz, ny, comps, own_rows)),
        out_shape=jax.ShapeDtypeStruct((own_rows, 1), F32),
        in_specs=[vmem, anywhere, anywhere, vmem, vmem, vmem, vmem],
        out_specs=vmem,
        scratch_shapes=[
            pltpu.VMEM((rows, modes), BF),
            pltpu.VMEM((n_member * shard, taps), BF),
            pltpu.VMEM((groups * cases, steps), BF),
            pltpu.VMEM((group_rows, modes), F32),
            pltpu.VMEM((taps, n_records * steps), BF),
            pltpu.VMEM((group_rows, n_records * steps), BF),
            pltpu.VMEM((groups * cases, steps), BF),
            pltpu.VMEM((n_mode - 1, slab, steps), BF),
            pltpu.VMEM((slab, steps), BF),
            pltpu.VMEM((n_member - 1, own_rows, steps), BF),
            dma((n_chunk,)),
            dma((2,)),
            dma((nz - 1,)),
            dma((nz - 1,)),
            dma((nz, ny - 1)),
            dma((nz, ny - 1)),
            dma((nz - 1,)),
            dma((nz - 1,)),
            dma((nz, ny - 1)),
            dma((nz, ny - 1)),
            dma((n_mode - 1,)),
            dma((n_mode - 1,)),
            dma((n_mode - 1,)),
            dma((n_mode - 1,)),
            dma((n_member - 1,)),
            dma((n_member - 1,)),
        ],
        compiler_params=pltpu.CompilerParams(
            collective_id=0, has_side_effects=True, vmem_limit_bytes=60 * 1024 * 1024
        ),
        cost_estimate=pl.CostEstimate(
            flops=2 * group_rows * rows * modes, bytes_accessed=2 * rows * modes, transcendentals=0
        ),
    )(accel, modal_kernel, mode_shapes, code, rec, mix, grav)
    return out.reshape(own_groups, cases)


def solution(mesh):
    placed = (
        P(),
        P(("mode", "member"), None),
        P("member", "mode"),
        P("member", None),
        P("member", None),
        P(("mode", "member"), None),
        P(),
        P(("mode", "member"), None),
    )
    return jax.shard_map(
        functools.partial(local, mesh.shape["mode"], mesh.shape["member"]),
        mesh=mesh,
        in_specs=placed,
        out_specs=P(("mode", "member"), None),
        check_vma=False,
    )
```

time: 462 us -> 49.9 us (0.11)
  local copies, waits for them, and re-layouts: 253 us -> 5.82 us
  waiting for transfers between devices: 166 us -> 0 us
  Pallas kernels: 0 us -> 40.4 us
  matrix products: 18.3 us -> 0 us
  between operations: 13.5 us -> 0.12 us
  starting transfers between devices: 8.14 us -> 0 us
    gather x2 -> x0, local copies, waits for them, and re-layouts: 245 us -> none  [lagged_table(): lag_table = ground_accel[:, offsets]]
    all_to_all x2 -> x0, waiting for transfers between devices: 71.8 us -> none  [the longest x1 71.8 us: local(): lax.all_to_all(outgoing.reshape(owner_total, slot_depth, -1).astype(jnp.b...]
    reduce_scatter x1 -> x0, waiting for transfers between devices: 52.1 us -> none  [local(): lax.psum_scatter(jnp.dot(mode_shapes, modal_resp, preferred_element_type=...]
    all_gather x1 -> x0, waiting for transfers between devices: 42.3 us -> none  [local(): modal_resp = lax.all_gather(local_resp, 'member', axis=0, tiled=True)]
    pallas_call x0 -> x1, Pallas kernels: none -> 40.4 us  [local(): pl.pallas_call(functools.partial(kernel, (n_mode, n_member, nz, ny, comps...]
    dot_general x5 -> x0, matrix products: 18.3 us -> none  [the longest x1 11.7 us: local(): jnp.dot(mode_shapes, modal_resp, preferred_element_type=jnp.float32)]
    all_to_all x2 -> x0, starting transfers between devices: 8.1 us -> none  [the longest x1 4.62 us: local(): lax.all_to_all(outgoing.reshape(owner_total, slot_depth, -1).astype(jnp.b...]
  transfers between devices with their start and end apart: 4 -> 0, of which waited for: 3 -> 0; matrix products, arithmetic and copies ran while one was open for 2% -> 0% of each run, Pallas kernels for 0% -> 0%
where the time goes in v1:
time: 49.9 us; the launch traced here: 49.6 us
  Pallas kernels  40.4 us (81%)
  local copies, waits for them, and re-layouts  5.82 us (12%)
  other arithmetic  3.3 us (7%)
    pallas_call x1, Pallas kernels, local(): pl.pallas_call(functools.partial(kernel, (n_mode, n_member, nz, ny, comps...  40.4 us
    mul x2, local copies, waits for them, and re-layouts, local(): mix = jnp.kron(jnp.eye(mix_groups, dtype=F32), case_coef)  2.22 us

profile of v1, /device:TPU:0, one launch (start us, length us, event | category | flops | bytes accessed | tf_op | source)
XLA Modules:
  0.0 49.6 jit_solution(4364991459295212698)
XLA Ops:
  0.0 0.8 %copy.14 = f32[8,6]{0,1:T(8,128)S(1)} copy(f32[8,6]{1,0:T(8,128)} %param.14) | data formatting | bytes 384 | tf_op args[6]
  0.8 0.5 broadcast_multiply_fusion
  1.2 0.0 copy-start.1
  1.2 0.0 copy-start.2
  1.3 0.0 copy-start.3
  1.3 0.0 copy-start
  1.3 0.0 copy-start.4
  1.3 2.1 %mul.54 = f32[1,256,192]{1,2,0:T(8,128)S(1)} reshape(f32[32,8,32,6]{1,0,3,2:T(8,128)S(1)} %broadcast_multiply_fusion) | data formatting | bytes 393216 | tf_op jit(solution)/shard_map/jit(kron)/mul | solution.py:306
  3.4 0.1 copy.17
  3.5 0.1 copy.16
  3.7 0.7 %pad_maximum_fusion.mix_ref = bf16[2,256,192]{2,1,0:T(8,128)(2,1)} fusion(bf16[1,256,192]{2,1,0:T(8,128)(2,1)S(1)} %subtract_convert_fusion, bf16[1,256,192]{2,1,0:T(8,128)(2,1)S(1)} %copy.17), kind=kLoop, calls=%fused_computation.1 | loop fusion | flops 98304 | bytes 393216 | tf_op jit(solution)/shard_map/stack | solution.py:308
  4.4 0.0 copy-done.1
  4.4 0.0 copy-done.2
  4.4 0.2 add.29
  4.6 0.3 add.30
  4.9 0.1 add.32
  5.1 0.6 %broadcast_add_fusion.code_ref = s32[8,768]{1,0:T(8,128)} fusion(s32[8,768]{1,0:T(8,128)S(1)} %add.30, s32[768]{0:T(1024)S(1)} %add.32), kind=kLoop, calls=%fused_computation.5 | loop fusion | flops 6144 | bytes 52224 | tf_op jit(solution)/shard_map/add | solution.py:303
  5.7 0.0 copy-done.3
  5.7 0.7 %reshape.66.grav_ref = f32[32,1]{1,0:T(8,128)} reshape(f32[4,8]{1,0:T(4,128)S(1)} %copy-done.3) | data formatting | bytes 256 | tf_op jit(solution)/shard_map/reshape | solution.py:309
  6.4 0.0 copy-done
  6.4 0.6 %pad_convert_fusion.accel_ref = f32[4,640]{1,0:T(4,128)} fusion(bf16[4,639]{1,0:T(4,128)(2,1)S(1)} %copy-done), kind=kLoop, calls=%fused_computation.6 | loop fusion | flops 2560 | bytes 15352 | tf_op jit(solution)/shard_map/jit(_pad)/pad | solution.py:301
  7.0 0.0 copy-done.4
  7.0 0.1 broadcast_in_dim.12
  7.1 0.7 %broadcast_in_dim.13.rec_ref = bf16[32,128]{1,0:T(8,128)(2,1)} broadcast(bf16[32]{0:T(256)(128)(2,1)S(1)} %broadcast_in_dim.12), dimensions={0} | broadcast | bytes 8256 | tf_op jit(solution)/shard_map/broadcast_in_dim | solution.py:304
  7.7 40.4 %shard_map.82 = f32[32,1]{1,0:T(8,128)} custom-call(f32[4,640]{1,0:T(4,128)} %pad_convert_fusion.accel_ref, bf16[128,512]{1,0:T(8,128)(2,1)} %kern_ref.1, bf16[6144,1024]{1,0:T(8,128)(2,1)} %shapes_ref.1, s32[8,768]{1,0:T(8,128)} %broadcast_add_fusion.code_ref, bf16[32,128]{1,0:T(8,128)(2,1)} %broadcast_in_dim.13.rec_ref, ...), custom_call_target="tpu_custom_call" | custom-call | flops 9663676416 | bytes 12582912 | tf_op jit(solution)/shard_map/pallas_call | solution.py:315
  48.1 0.8 %reduce = f32[32]{0:T(128)S(1)} reduce(f32[32,1]{1,0:T(8,128)} %shard_map.82, f32[]{:T(128)} %constant.12), dimensions={1}, to_apply=%pallas_call.3.reduce_sub_computation | reduce | bytes 260 | tf_op jit(solution)/shard_map/pallas_call | solution.py:315
  48.9 0.7 %reshape.65 = f32[4,8]{1,0:T(4,128)} reshape(f32[32]{0:T(128)S(1)} %reduce) | data formatting | bytes 256 | tf_op jit(solution)/shard_map/reshape | solution.py:355
  (6 shorter events, 0.1 us)
Async XLA Ops:
  1.2 3.2 %copy-start.1 = (s32[1024,1]{0,1:T(1,128)S(1)}, s32[1024,1]{0,1:T(1,128)}, u32[]{:S(2)}) copy-start(s32[1024,1]{0,1:T(1,128)} %param.12) | copy-start | bytes 12292
  1.2 3.2 %copy-start.2 = (s32[1024,1]{0,1:T(1,128)S(1)}, s32[1024,1]{0,1:T(1,128)}, u32[]{:S(2)}) copy-start(s32[1024,1]{0,1:T(1,128)} %param.11) | copy-start | bytes 12292
  1.3 4.4 %copy-start.3 = (f32[4,8]{1,0:T(4,128)S(1)}, f32[4,8]{1,0:T(4,128)}, u32[]{:S(2)}) copy-start(f32[4,8]{1,0:T(4,128)} %param.15) | copy-start | bytes 388
  1.3 5.1 %copy-start = (bf16[4,639]{1,0:T(4,128)(2,1)S(1)}, bf16[4,639]{1,0:T(4,128)(2,1)}, u32[]{:S(2)}) copy-start(bf16[4,639]{1,0:T(4,128)(2,1)} %param.8) | copy-start | bytes 15340
  1.3 5.7 %copy-start.4 = (s32[4,8]{1,0:T(4,128)S(1)}, s32[4,8]{1,0:T(4,128)}, u32[]{:S(2)}) copy-start(s32[4,8]{1,0:T(4,128)} %param.13) | copy-start | bytes 388

commit v2 on v1

--- a/solution.py
+++ b/solution.py
@@ -17,9 +17,10 @@
     accel_ref,
     kern_ref,
     shapes_ref,
-    code_ref,
-    rec_ref,
-    mix_ref,
+    owner_ref,
+    group_ref,
+    table_ref,
+    coef_ref,
     grav_ref,
     out_ref,
     mbuf,
@@ -32,6 +33,10 @@
     abuf,
     ybuf,
     bbuf,
+    mix_ref,
+    padded,
+    code_ref,
+    rec_ref,
     msem,
     loc_sem,
     z_send,
@@ -68,6 +73,13 @@
     for i in range(n_chunk):
         load(i).start()
 
+    table = table_ref[...].astype(F32)
+    rec_ref[...] = (
+        jnp.broadcast_to(table[:, :, None], table.shape + (rec_ref.shape[1],))
+        .reshape(rec_ref.shape)
+        .astype(BF)
+    )
+
     def member_at(zz, yy):
         return zz * ny + yy
 
@@ -140,14 +152,40 @@
         z_copies[d].start()
 
     steps = lagged.shape[1] // n_records
+    span = accel_ref.shape[1]
+    padded[...] = jnp.zeros_like(padded)
+    padded[:, :span] = accel_ref[...].astype(F32)
     for r in range(n_records):
         for q in range(taps // steps):
             start = taps - steps * (q + 1)
-            piece = jnp.broadcast_to(accel_ref[r : r + 1, start : start + 2 * steps], (steps, 2 * steps))
+            piece = jnp.broadcast_to(padded[r : r + 1, start : start + 2 * steps], (steps, 2 * steps))
             rolled = pltpu.roll(piece, steps + 1, 1, stride=1, stride_axis=0)
             lagged[q * steps : (q + 1) * steps, r * steps : (r + 1) * steps] = rolled[
                 :, :steps
             ].astype(BF)
+
+    cases = coef_ref.shape[0]
+    mixed_rows, mixed_from = mix_ref.shape[1:]
+    stacked = jnp.concatenate([coef_ref[...]] * (mixed_rows // cases), axis=0)
+    at_row = lax.broadcasted_iota(jnp.int32, (mixed_rows, mixed_from), 0) // cases
+    offset = lax.broadcasted_iota(jnp.int32, (mixed_rows, mixed_from), 1) - comps * at_row
+    mix = jnp.zeros((mixed_rows, mixed_from), F32)
+    for c in range(comps):
+        mix = jnp.where(offset == c, stacked[:, c : c + 1], mix)
+    mix_ref[0] = mix.astype(BF)
+    mix_ref[1] = (mix - mix.astype(BF).astype(F32)).astype(BF)
+
+    wide = (chunk // comps, chunk)
+    place = lax.broadcasted_iota(jnp.int32, wide, 1) - comps * lax.broadcasted_iota(
+        jnp.int32, wide, 0
+    )
+    inside = (place >= 0) & (place < comps)
+    spread = jnp.where(inside, 1.0, 0.0).astype(BF)
+    comp = jnp.sum(jnp.where(inside, place, 0), axis=0, keepdims=True).astype(F32)
+    owners = jnp.dot(owner_ref[...].astype(F32).astype(BF), spread, preferred_element_type=F32)
+    groups = jnp.dot(group_ref[...].astype(F32).astype(BF), spread, preferred_element_type=F32)
+    own_groups = table_ref.shape[0]
+    code_ref[...] = ((owners * own_groups + groups) * comps + comp).astype(jnp.int32)
 
     acc[...] = jnp.zeros_like(acc)
     part = chunk if group_rows % chunk == 0 else group_rows
@@ -208,8 +246,6 @@
     lax.fori_loop(0, group_rows // part, contract, 0)
     for copy in mr_copies:
         copy.wait_recv()
-
-    mixed_rows, mixed_from = mix_ref.shape[1:]
 
     def mix_slab(target):
         for k in range(slab // mixed_rows):
@@ -263,7 +299,10 @@
     for d, copy in enumerate(b_copies):
         copy.wait_recv()
         own = own + bbuf[d].astype(F32)
-    out_ref[...] = jnp.max(jnp.abs(own + grav_ref[...]), axis=1, keepdims=True)
+    own = own.reshape(own_rows // cases, cases, steps)
+    top = grav_ref[...] + jnp.max(own, axis=2)
+    bottom = grav_ref[...] + jnp.min(own, axis=2)
+    out_ref[...] = jnp.maximum(top, -bottom)
 
     for copies in (z_copies, zr_copies, y_copies, yr_copies):
         for copy in copies.values():
@@ -298,15 +337,8 @@
     n_chunk = rows // chunk
     group_rows = groups * comps
 
-    accel = jnp.pad(ground_accel.astype(F32), ((0, 0), (0, taps + steps - span)))
-    group = (member_owner * own_groups + member_group) * comps
-    code = (group + jnp.arange(comps)[None, :]).reshape(n_chunk, chunk)
-    rec = jnp.broadcast_to(record_table.astype(BF).reshape(own_rows, 1), (own_rows, steps))
+    by_chunk = (n_chunk, chunk // comps)
     mix_groups = 32
-    mix = jnp.kron(jnp.eye(mix_groups, dtype=F32), case_coef)
-    high = mix.astype(BF)
-    mix = jnp.stack([high, (mix - high.astype(F32)).astype(BF)])
-    grav = gravity.reshape(own_rows, 1)
 
     vmem = pl.BlockSpec(memory_space=pltpu.VMEM)
     anywhere = pl.BlockSpec(memory_space=pl.ANY)
@@ -314,8 +346,8 @@
     slab = n_member * own_rows
     out = pl.pallas_call(
         functools.partial(kernel, (n_mode, n_member, nz, ny, comps, own_rows)),
-        out_shape=jax.ShapeDtypeStruct((own_rows, 1), F32),
-        in_specs=[vmem, anywhere, anywhere, vmem, vmem, vmem, vmem],
+        out_shape=jax.ShapeDtypeStruct((own_groups, cases), F32),
+        in_specs=[vmem, anywhere, anywhere, vmem, vmem, vmem, vmem, vmem],
         out_specs=vmem,
         scratch_shapes=[
             pltpu.VMEM((rows, modes), BF),
@@ -328,6 +360,10 @@
             pltpu.VMEM((n_mode - 1, slab, steps), BF),
             pltpu.VMEM((slab, steps), BF),
             pltpu.VMEM((n_member - 1, own_rows, steps), BF),
+            pltpu.VMEM((2, mix_groups * cases, mix_groups * comps), BF),
+            pltpu.VMEM((n_records, taps + steps), F32),
+            pltpu.VMEM((n_chunk, chunk), jnp.int32),
+            pltpu.VMEM((own_rows, steps), BF),
             dma((n_chunk,)),
             dma((2,)),
             dma((nz - 1,)),
@@ -351,8 +387,17 @@
         cost_estimate=pl.CostEstimate(
             flops=2 * group_rows * rows * modes, bytes_accessed=2 * rows * modes, transcendentals=0
         ),
-    )(accel, modal_kernel, mode_shapes, code, rec, mix, grav)
-    return out.reshape(own_groups, cases)
+    )(
+        ground_accel,
+        modal_kernel,
+        mode_shapes,
+        member_owner.reshape(by_chunk),
+        member_group.reshape(by_chunk),
+        record_table,
+        case_coef,
+        gravity,
+    )
+    return out
 
 
 def solution(mesh):

time: 49.9 us -> 41.6 us (0.83)
  local copies, waits for them, and re-layouts: 5.82 us -> 1.26 us
  other arithmetic: 3.3 us -> 0 us
    mul x2 -> x0, local copies, waits for them, and re-layouts: 2.22 us -> none  [local(): mix = jnp.kron(jnp.eye(mix_groups, dtype=F32), case_coef)]
    reshape x2 -> x0, local copies, waits for them, and re-layouts: 1.34 us -> none  [the longest x1 0.68 us: local(): grav = gravity.reshape(own_rows, 1)]
    pallas_call x1 -> x0, other arithmetic: 0.83 us -> none  [local(): pl.pallas_call(functools.partial(kernel, (n_mode, n_member, nz, ny, comps...]
    broadcast_in_dim x2 -> x0, local copies, waits for them, and re-layouts: 0.76 us -> none  [local(): jnp.broadcast_to(record_table.astype(BF).reshape(own_rows, 1), (own_rows,...]
    another operation x1 -> x0, other arithmetic: 0.74 us -> none  [local(): mix = jnp.stack([high, (mix - high.astype(F32)).astype(BF)])]
    add x1 -> x0, other arithmetic: 0.62 us -> none  [local(): code = (group + jnp.arange(comps)[None, :]).reshape(n_chunk, chunk)]
    pad x1 -> x0, other arithmetic: 0.6 us -> none  [local(): jnp.pad(ground_accel.astype(F32), ((0, 0), (0, taps + steps - span)))]
    add x4 -> x0, local copies, waits for them, and re-layouts: 0.6 us -> none  [local(): code = (group + jnp.arange(comps)[None, :]).reshape(n_chunk, chunk)]
where the time goes in v2:
time: 41.6 us; the launch traced here: 41.4 us
  Pallas kernels  40.1 us (96%)
  local copies, waits for them, and re-layouts  1.26 us (3%)
    pallas_call x1, Pallas kernels, local(): pl.pallas_call(functools.partial(kernel, (n_mode, n_member, nz, ny, comps...  40.1 us
    unnamed x1, local copies, waits for them, and re-layouts  1.26 us

profile of v2, /device:TPU:0, one launch (start us, length us, event | category | flops | bytes accessed | tf_op | source)
XLA Modules:
  0.0 41.4 jit_solution(916065330260783759)
XLA Ops:
  0.0 40.1 %shard_map.82 = f32[4,8]{1,0:T(4,128)} custom-call(bf16[4,639]{1,0:T(4,128)(2,1)} %accel_ref.1, bf16[128,512]{1,0:T(8,128)(2,1)} %kern_ref.1, bf16[6144,1024]{1,0:T(8,128)(2,1)} %shapes_ref.1, s32[8,128]{1,0:T(8,128)} %bitcast.2, s32[8,128]{1,0:T(8,128)} %bitcast.3, s32[4,8]{1,0:T(4,128)} %table_ref.1, f32[8,6]{1,0:T(8,128)} %coef_ref.1, f32[4,8]{1,0:T(4,128)} %grav_ref.1), custom_call_target="tpu_custom_call" | custom-call | flops 9663676416 | bytes 12582912 | tf_op jit(solution)/shard_map/pallas_call | solution.py:347
  40.1 1.3 %copy.10 = f32[4,8]{1,0:T(4,128)} copy(f32[4,8]{1,0:T(4,128)} %shard_map.82) | data formatting | bytes 256

commit v3 on v2

--- a/solution.py
+++ b/solution.py
@@ -36,6 +36,8 @@
     mix_ref,
     padded,
     code_ref,
+    order_ref,
+    perm,
     rec_ref,
     msem,
     loc_sem,
@@ -58,7 +60,8 @@
     n_records = accel_ref.shape[0]
     taps = kern_ref.shape[1]
     shard = kern_ref.shape[0]
-    n_chunk, chunk = code_ref.shape
+    n_chunk, chunk_members = owner_ref.shape
+    chunk = chunk_members * comps
     group_rows = acc.shape[0]
     mode = lax.axis_index("mode")
     member = lax.axis_index("member")
@@ -168,43 +171,48 @@
     mixed_rows, mixed_from = mix_ref.shape[1:]
     stacked = jnp.concatenate([coef_ref[...]] * (mixed_rows // cases), axis=0)
     at_row = lax.broadcasted_iota(jnp.int32, (mixed_rows, mixed_from), 0) // cases
-    offset = lax.broadcasted_iota(jnp.int32, (mixed_rows, mixed_from), 1) - comps * at_row
+    mixed_groups = mixed_from // comps
+    offset = lax.broadcasted_iota(jnp.int32, (mixed_rows, mixed_from), 1) - at_row
     mix = jnp.zeros((mixed_rows, mixed_from), F32)
     for c in range(comps):
-        mix = jnp.where(offset == c, stacked[:, c : c + 1], mix)
+        mix = jnp.where(offset == c * mixed_groups, stacked[:, c : c + 1], mix)
     mix_ref[0] = mix.astype(BF)
     mix_ref[1] = (mix - mix.astype(BF).astype(F32)).astype(BF)
 
-    wide = (chunk // comps, chunk)
-    place = lax.broadcasted_iota(jnp.int32, wide, 1) - comps * lax.broadcasted_iota(
-        jnp.int32, wide, 0
-    )
-    inside = (place >= 0) & (place < comps)
-    spread = jnp.where(inside, 1.0, 0.0).astype(BF)
-    comp = jnp.sum(jnp.where(inside, place, 0), axis=0, keepdims=True).astype(F32)
-    owners = jnp.dot(owner_ref[...].astype(F32).astype(BF), spread, preferred_element_type=F32)
-    groups = jnp.dot(group_ref[...].astype(F32).astype(BF), spread, preferred_element_type=F32)
-    own_groups = table_ref.shape[0]
-    code_ref[...] = ((owners * own_groups + groups) * comps + comp).astype(jnp.int32)
+    code_ref[...] = owner_ref[...] * table_ref.shape[0] + group_ref[...]
+    few = order_ref.shape[0] // comps
+    to_row = lax.broadcasted_iota(jnp.int32, order_ref.shape, 0)
+    from_row = lax.broadcasted_iota(jnp.int32, order_ref.shape, 1)
+    wanted_row = comps * (to_row - few * (to_row // few)) + to_row // few
+    order_ref[...] = jnp.where(from_row == wanted_row, 1.0, 0.0).astype(BF)
 
     acc[...] = jnp.zeros_like(acc)
-    part = chunk if group_rows % chunk == 0 else group_rows
+    part = 128 * comps
+    groups = group_rows // comps
 
     def chunk_step(i, carry):
         load(i).wait()
         code = code_ref[pl.ds(i, 1), :]
-        block = mbuf[pl.ds(pl.multiple_of(i * chunk, chunk), chunk), :]
-
-        def row_step(p, inner):
-            first = pl.multiple_of(p * part, part)
-            rows = lax.broadcasted_iota(jnp.int32, (part, chunk), 0) + first
-            hot = jnp.where(rows == code, 1.0, 0.0).astype(BF)
-            acc[pl.ds(first, part), :] += jnp.dot(hot, block, preferred_element_type=F32)
-            return inner
-
-        return lax.fori_loop(0, group_rows // part, row_step, carry)
-
-    marks = [(n_chunk * (d + 1)) // (nz + 1) for d in range(1, nz)]
+        hot = jnp.where(
+            lax.broadcasted_iota(jnp.int32, (groups, chunk_members), 0) == code, 1.0, 0.0
+        ).astype(BF)
+        size = few * comps
+        for k in range(chunk // size):
+            rows = pl.ds(pl.multiple_of(i * chunk + k * size, size), size)
+            ordered = jnp.dot(order_ref[...], mbuf[rows, :], preferred_element_type=F32).astype(BF)
+            for c in range(comps):
+                perm[pl.ds(c * chunk_members + k * few, few), :] = ordered[
+                    c * few : (c + 1) * few
+                ]
+        for c in range(comps):
+            acc[pl.ds(c * groups, groups), :] += jnp.dot(
+                hot,
+                perm[pl.ds(c * chunk_members, chunk_members), :],
+                preferred_element_type=F32,
+            )
+        return carry
+
+    marks = [(n_chunk * d) // nz for d in range(1, nz)]
     done = 0
     for d in range(1, nz):
         lax.fori_loop(done, marks[d - 1], chunk_step, 0)
@@ -252,8 +260,16 @@
             to = pl.ds(
                 pl.multiple_of(target * slab + k * mixed_rows, mixed_rows), mixed_rows
             )
-            start = (target * (slab // mixed_rows) + k) * mixed_from
-            got = sums[pl.ds(pl.multiple_of(start, mixed_from), mixed_from), :]
+            start = (target * (slab // mixed_rows) + k) * mixed_groups
+            got = jnp.concatenate(
+                [
+                    sums[
+                        pl.ds(pl.multiple_of(start + c * groups, mixed_groups), mixed_groups), :
+                    ]
+                    for c in range(comps)
+                ],
+                axis=0,
+            )
             mixed = jnp.dot(mix_ref[0], got, preferred_element_type=F32) + jnp.dot(
                 mix_ref[1], got, preferred_element_type=F32
             )
@@ -333,7 +349,7 @@
     own_rows = own_groups * cases
     groups = n_mode * n_member * own_groups
     rows, modes = mode_shapes.shape
-    chunk = 128 * comps
+    chunk = 256 * comps
     n_chunk = rows // chunk
     group_rows = groups * comps
 
@@ -362,7 +378,9 @@
             pltpu.VMEM((n_member - 1, own_rows, steps), BF),
             pltpu.VMEM((2, mix_groups * cases, mix_groups * comps), BF),
             pltpu.VMEM((n_records, taps + steps), F32),
-            pltpu.VMEM((n_chunk, chunk), jnp.int32),
+            pltpu.VMEM((n_chunk, chunk // comps), jnp.int32),
+            pltpu.VMEM((32 * comps, 32 * comps), BF),
+            pltpu.VMEM((chunk, modes), BF),
             pltpu.VMEM((own_rows, steps), BF),
             dma((n_chunk,)),
             dma((2,)),

time: 41.6 us -> 45.9 us (1.10)
  other arithmetic: 0 us -> 2.69 us
  local copies, waits for them, and re-layouts: 1.26 us -> 2.94 us
    unnamed x0 -> x2, other arithmetic: none -> 2.69 us
    reshape x0 -> x2, local copies, waits for them, and re-layouts: none -> 1.2 us  [the longest x1 0.6 us: local(): member_owner.reshape(by_chunk)]
    unnamed x1 -> x2, local copies, waits for them, and re-layouts: 1.26 us -> 1.74 us
where the time goes in v3:
time: 45.9 us; the launch traced here: 45.6 us
  Pallas kernels  40 us (87%)
  local copies, waits for them, and re-layouts  2.94 us (6%)
  other arithmetic  2.69 us (6%)
    pallas_call x1, Pallas kernels, local(): pl.pallas_call(functools.partial(kernel, (n_mode, n_member, nz, ny, comps...  40 us
    unnamed x2, other arithmetic  2.69 us
    unnamed x2, local copies, waits for them, and re-layouts  1.74 us

profile of v3, /device:TPU:0, one launch (start us, length us, event | category | flops | bytes accessed | tf_op | source)
XLA Modules:
  0.0 45.6 jit_solution(10266537695729713763)
XLA Ops:
  0.0 0.5 %broadcast.6 = s32[]{:T(128)} broadcast(s32[]{:T(128)} %constant.8), dimensions={} | broadcast | bytes 8 | tf_op args[3]
  0.5 1.3 %reduce.6 = s32[1024]{0:T(1024)S(1)} reduce(s32[1024,1]{0,1:T(1,128)} %param.11, s32[]{:T(128)} %broadcast.6), dimensions={1}, to_apply=%param.11.reduce_sub_computation.3 | reduce | bytes 8196 | tf_op args[3]
  1.9 0.6 %reshape.6.owner_ref = s32[4,256]{1,0:T(4,128)} reshape(s32[1024]{0:T(1024)S(1)} %reduce.6) | data formatting | bytes 8192 | tf_op jit(solution)/shard_map/reshape | solution.py:412
  2.5 1.3 %reduce.7 = s32[1024]{0:T(1024)S(1)} reduce(s32[1024,1]{0,1:T(1,128)} %param.12, s32[]{:T(128)} %broadcast.6), dimensions={1}, to_apply=%param.12.reduce_sub_computation.3 | reduce | bytes 8196 | tf_op args[4]
  3.8 0.6 %reshape.7.group_ref = s32[4,256]{1,0:T(4,128)} reshape(s32[1024]{0:T(1024)S(1)} %reduce.7) | data formatting | bytes 8192 | tf_op jit(solution)/shard_map/reshape | solution.py:413
  4.4 40.0 %shard_map.82 = f32[4,8]{1,0:T(4,128)} custom-call(bf16[4,639]{1,0:T(4,128)(2,1)} %accel_ref.1, bf16[128,512]{1,0:T(8,128)(2,1)} %kern_ref.1, bf16[6144,1024]{1,0:T(8,128)(2,1)} %shapes_ref.1, s32[4,256]{1,0:T(4,128)} %reshape.6.owner_ref, s32[4,256]{1,0:T(4,128)} %reshape.7.group_ref, s32[4,8]{1,0:T(4,128)} %table_ref.1, f32[8,6]{1,0:T(8,128)} %coef_ref.1, ...), custom_call_target="tpu_custom_call" | custom-call | flops 9663676416 | bytes 12582912 | tf_op jit(solution)/shard_map/pallas_call | solution.py:363
  44.4 1.2 %copy.10 = f32[4,8]{1,0:T(4,128)} copy(f32[4,8]{1,0:T(4,128)} %shard_map.82) | data formatting | bytes 256
